TPU v7x, 32 devices: a whole 2x2x4 slice. The times are simulated.
32 devices in a mesh: band: 2 (over x), stn: 8 (over z, y), tm: 2 (over core).
Axes of the slice: x: 2, y: 2, z: 4, core: 2. Of those that a mesh axis runs over, the one named last changes fastest.
Arguments:
- voltages: int32 [704, 4, 32768], P('stn', 'band', 'tm'), parts along dimension 1, may hold values from -125 to 125, as said below
- filter_taps: float32 [16, 128], replicated, may hold values from -0.036 to 0.036
Outputs:
- visibilities: float32 [2, 2, 128, 704, 704], P(None, None, ('band', 'stn', 'tm')), parts along dimension 2
There are 2 independent parts, one for each index of `band`. A program takes and returns all parts, laid end to end along the dimension named above; an argument that names none is the same for every part. Nothing has to cross between parts.
Inputs may be any that keep to these rules, and one draw needn't show every extreme that they name: `voltages`: each input's samples are an integer gain of -2 to 2 times a signal common to all inputs plus noise of its own.
All inputs are finite; a program needn't handle non-finite values.
Results may differ from a plain program's by a relative error of at most 0.00049.
Values may be sent and summed in bfloat16 or wider, within the bound.
A program may use at most 192 MiB of HBM per device.

v0:
```python
import math

import jax
import jax.numpy as jnp
from jax import lax
from jax.sharding import PartitionSpec as P


def passed_along(value, axis, steps):
    count = lax.axis_size(axis)
    pairs = [(source, (source + steps) % count) for source in range(count)]
    return lax.ppermute(value, axis, pairs)


def transform_table(frame_len, chan_count):
    sample_index = jnp.arange(frame_len, dtype=jnp.int32)[:, None]
    chan_index = jnp.arange(chan_count, dtype=jnp.int32)[None, :]
    phase = (2 * chan_index + 1) * sample_index % (2 * frame_len)
    angle = phase.astype(jnp.float32) * (math.pi / frame_len)
    factor = 1.0 / math.sqrt(frame_len)
    cosine = jnp.cos(angle) * factor
    sine = -jnp.sin(angle) * factor
    return jnp.stack([cosine, sine], axis=2).reshape(frame_len, 2 * chan_count)


def arrange(blocks):
    stations, blocks_time, per_dev, parts_two, inputs_dev, sub_count, spec_dev = blocks.shape
    ordered = jnp.transpose(blocks, (3, 5, 2, 0, 4, 1, 6))
    return ordered.reshape(
        parts_two, sub_count, per_dev, stations * inputs_dev, blocks_time * spec_dev
    )


def correlate(stacked):
    real_in = stacked[0]
    imag_in = stacked[1]
    right_side = jnp.concatenate([real_in, imag_in], axis=-1)
    left_imag = jnp.concatenate([imag_in, -real_in], axis=-1)
    real_part = jnp.einsum(
        "gcis,gcjs->gcij", right_side, right_side, preferred_element_type=jnp.float32
    )
    imag_part = jnp.einsum(
        "gcis,gcjs->gcij", left_imag, right_side, preferred_element_type=jnp.float32
    )
    return jnp.stack([real_part, imag_part])


def shards(voltages, filter_taps):
    inputs_dev, sub_count, time_dev = voltages.shape
    taps_count, frame_len = filter_taps.shape
    spec_dev = time_dev // frame_len
    chan_count = frame_len // 2
    lagging = taps_count - 1
    frames = voltages.astype(jnp.bfloat16).reshape(inputs_dev, sub_count, spec_dev, frame_len)
    last_frames = frames[:, :, spec_dev - lagging :, :]
    received = passed_along(last_frames, "tm", 1)
    earlier = jnp.concatenate([jnp.zeros_like(received[:, :1]), received[:, :-1]], axis=1)
    history = jnp.where(lax.axis_index("tm") == 0, earlier, received)
    extended = jnp.concatenate([history, frames], axis=2).astype(jnp.float32)
    filtered = filter_taps[0] * extended[:, :, 0:spec_dev]
    for tap_index in range(1, taps_count):
        filtered = (
            filtered + filter_taps[tap_index] * extended[:, :, tap_index : tap_index + spec_dev]
        )
    table = transform_table(frame_len, chan_count)
    spectra = lax.dot_general(
        table,
        filtered.reshape(-1, frame_len),
        (((0,), (1,)), ((), ())),
        precision=lax.Precision.HIGHEST,
        preferred_element_type=jnp.float32,
    ).astype(jnp.bfloat16)
    stations = lax.axis_size("stn")
    halves = lax.axis_size("tm")
    scale = 1.0 / (spec_dev * halves)
    moved = lax.all_to_all(spectra[None], ("stn", "tm"), split_axis=1, concat_axis=0, tiled=True)
    per_dev = moved.shape[1] // 2
    blocks = moved.reshape(stations, halves, per_dev, 2, inputs_dev, sub_count, spec_dev)
    result = correlate(arrange(blocks))
    return result * scale


def solution(mesh):
    placed = (P("stn", "band", "tm"), P())
    return jax.shard_map(
        shards,
        mesh=mesh,
        in_specs=placed,
        out_specs=P(None, None, ("band", "stn", "tm"), None, None),
        check_vma=False,
    )
```

profile of v0, /device:TPU:0, one launch (start us, length us, event | category | flops | bytes accessed | tf_op | source)
XLA Modules:
  0.0 507.4 jit_solution(10586503539075918280)
XLA Ops:
  0.0 9.0 %convert_element_type.26 = bf16[88,2,16384]{2,1,0:T(2,128)(2,1)} convert(s32[88,2,16384]{2,1,0:T(2,128)} %param.2) | non-fusion elementwise | flops 2883584 | bytes 17301504 | tf_op jit(solution)/shard_map/convert_element_type | solution.py:54
  9.0 0.0 copy-start.1
  9.0 10.5 %reshape.154 = bf16[88,2,128,128]{3,2,1,0:T(8,128)(2,1)} reshape(bf16[88,2,16384]{2,1,0:T(2,128)(2,1)} %convert_element_type.26) | data formatting | bytes 11534336 | tf_op jit(solution)/shard_map/reshape | solution.py:54
  19.5 1.4 slice.146
  20.9 0.1 copy.33
  21.1 0.2 copy.19
  21.3 0.5 collective-permute-start
  21.8 0.2 cosine_multiply_fusion
  22.0 0.1 copy.17
  22.1 0.0 copy-done.1
  22.1 1.4 collective-permute-done
  23.6 0.1 copy.28
  23.6 0.2 pad_select_fusion
  23.8 10.6 %maximum_convert_fusion = f32[88,2,143,128]{3,2,0,1:T(8,128)} fusion(bf16[88,2,15,128]{3,2,0,1:T(8,128)(2,1)S(1)} %pad_select_fusion, bf16[88,2,128,128]{3,2,1,0:T(8,128)(2,1)} %reshape.154), kind=kLoop, calls=%fused_computation.36 | loop fusion | flops 12886016 | bytes 19329024 | tf_op jit(solution)/shard_map/convert_element_type | solution.py:59
  34.4 74.6 %fusion.1 = f32[88,2,128,128]{3,2,0,1:T(8,128)} fusion(f32[88,2,143,128]{3,2,0,1:T(8,128)} %maximum_convert_fusion, f32[128]{0:T(128)S(1)} %get-tuple-element.23, f32[128]{0:T(128)S(1)} %get-tuple-element.24, f32[128]{0:T(128)S(1)} %get-tuple-element.10, f32[128]{0:T(128)S(1)} %get-tuple-element.11, f32[128]{0:T(128)S(1)} %get-tuple-element.12, ...), kind=kLoop, calls=%fused_computation.4 | loop fusion | flops 89391104 | bytes 196091904 | tf_op jit(solution)/shard_map/add | solution.py:63
  109.0 10.6 %copy.22 = f32[88,2,128,128]{3,2,1,0:T(8,128)} copy(f32[88,2,128,128]{3,2,0,1:T(8,128)} %fusion.1) | data formatting | bytes 23068672 | tf_op jit(solution)/shard_map/add | solution.py:63
  119.7 13.3 %fusion = bf16[1,128,22528]{2,1,0:T(8,128)(2,1)S(1)} fusion(f32[128,128]{0,1:T(8,128)S(1)} %bitcast.54, f32[22528,128]{1,0:T(8,128)} %bitcast.52), kind=kOutput, calls=%fused_computation.2 | convolution fusion | flops 4432068608 | bytes 17367040 | tf_op jit(solution)/shard_map/dot_general | solution.py:66
  132.9 47.5 %copy.32 = bf16[1,128,22528]{2,0,1:T(2,128)(2,1)} copy(bf16[1,128,22528]{2,1,0:T(8,128)(2,1)S(1)} %fusion) | data formatting | bytes 11534336 | tf_op jit(solution)/shard_map/broadcast_in_dim | solution.py:76
  180.5 0.6 broadcast.142
  181.0 35.9 %reduce.2 = bf16[128,22528]{1,0:T(8,128)(2,1)} reduce(bf16[128,1,22528]{2,1,0:T(2,128)(2,1)} %bitcast.51, bf16[]{:T(256)} %broadcast.142), dimensions={1}, to_apply=%bitcast.50.reduce_sub_computation | reduce | bytes 11534338
  216.9 13.4 %reshape.156 = bf16[16,2,90112]{2,1,0:T(2,128)(2,1)} reshape(bf16[128,22528]{1,0:T(8,128)(2,1)} %reduce.2) | data formatting | bytes 11534336
  230.3 133.6 %all_to_all.4 = bf16[16,2,90112]{2,1,0:T(2,128)(2,1)} all-to-all(bf16[16,2,90112]{2,1,0:T(2,128)(2,1)} %reshape.156), channel_id=1, replica_groups=mesh['band'=2,'stn'=8,'tm'=2] {'stn','tm'}, dimensions={0} | all-to-all | bytes 11534336 | tf_op jit(solution)/shard_map/all_to_all | solution.py:76
  363.9 13.8 %reshape.157 = bf16[128,1,22528]{2,1,0:T(2,128)(2,1)} reshape(bf16[16,2,90112]{2,1,0:T(2,128)(2,1)} %all_to_all.4) | data formatting | bytes 11534336
  377.7 36.0 %bitcast_reduce_fusion = bf16[128,22528]{1,0:T(8,128)(2,1)} fusion(bf16[128,1,22528]{2,1,0:T(2,128)(2,1)} %reshape.157), kind=kLoop, calls=%fused_computation.75 | loop fusion | bytes 11534336 | tf_op jit(solution)/shard_map/all_to_all | solution.py:76
  413.7 8.9 %reshape.153 = bf16[8,2,4,2,88,2,128]{6,5,4,3,2,1,0:T(2,128)(2,1)} reshape(bf16[128,22528]{1,0:T(8,128)(2,1)} %bitcast_reduce_fusion) | data formatting | bytes 11534336 | tf_op jit(solution)/shard_map/reshape | solution.py:78
  422.6 8.4 %fusion.26 = (bf16[1,2,4,8,88,2,128]{6,1,4,0,2,5,3:T(2,128)(2,1)S(1)}, bf16[1,2,4,8,88,2,128]{6,1,4,0,2,5,3:T(2,128)(2,1)}) fusion(bf16[2,2,4,8,88,2,128]{6,1,4,0,2,5,3:T(2,128)(2,1)} %bitcast.53), kind=kLoop, calls=%fused_computation.73 | loop fusion | bytes 11534336 | tf_op jit(solution)/shard_map/slice | solution.py:36
  431.1 4.5 copy.25
  435.6 6.6 %squeeze.7 = bf16[2,4,704,256]{3,2,1,0:T(8,128)(2,1)S(1)} reshape(bf16[1,2,4,8,88,2,128]{6,5,4,3,2,1,0:T(2,128)(2,1)} %copy.25) | data formatting | bytes 5767168 | tf_op jit(solution)/shard_map/squeeze | solution.py:36
  442.2 6.4 %copy.24 = bf16[1,2,4,8,88,2,128]{6,5,4,3,2,1,0:T(2,128)(2,1)} copy(bf16[1,2,4,8,88,2,128]{6,1,4,0,2,5,3:T(2,128)(2,1)} %get-tuple-element.6) | data formatting | bytes 5767168 | tf_op jit(solution)/shard_map/slice | solution.py:35
  448.6 7.4 %squeeze.6 = bf16[2,4,704,256]{3,2,1,0:T(8,128)(2,1)} reshape(bf16[1,2,4,8,88,2,128]{6,5,4,3,2,1,0:T(2,128)(2,1)} %copy.24) | data formatting | bytes 5767168 | tf_op jit(solution)/shard_map/squeeze | solution.py:35
  456.0 5.0 fusion.27
  461.1 0.2 constant_dynamic-update-slice_fusion
  461.3 0.0 copy-start
  461.3 8.4 %convolution_bitcast_fusion.1 = f32[1,2,4,704,704]{4,3,2,1,0:T(8,128)} fusion(bf16[2,4,704,512]{3,2,1,0:T(8,128)(2,1)S(1)} %constant_dynamic-update-slice_fusion), kind=kOutput, calls=%fused_computation.35 | convolution fusion | flops 4060086272 | bytes 21626880 | tf_op jit(solution)/shard_map/gcis,gcjs->gcij/dot_general | solution.py:39
  469.7 0.0 copy-done
  469.7 14.1 %convolution_bitcast_fusion = f32[1,2,4,704,704]{4,3,2,1,0:T(8,128)} fusion(bf16[2,4,704,512]{3,2,1,0:T(8,128)(2,1)} %copy-done, bf16[2,4,704,256]{3,2,1,0:T(8,128)(2,1)} %get-tuple-element.7, bf16[2,4,704,256]{3,2,1,0:T(8,128)(2,1)S(1)} %squeeze.7), kind=kOutput, calls=%fused_computation.34 | convolution fusion | flops 4071620608 | bytes 27394048 | tf_op jit(solution)/shard_map/gcis,gcjs->gcij/dot_general | solution.py:42
  483.8 23.2 %maximum_multiply_fusion = f32[2,2,4,704,704]{4,3,2,1,0:T(8,128)} fusion(f32[1,2,4,704,704]{4,3,2,1,0:T(8,128)} %convolution_bitcast_fusion, f32[1,2,4,704,704]{4,3,2,1,0:T(8,128)} %convolution_bitcast_fusion.1), kind=kLoop, calls=%fused_computation | loop fusion | flops 15859712 | bytes 63438848 | tf_op jit(solution)/shard_map/mul | solution.py:80
  (4 shorter events, 0.0 us)
Async XLA Ops:
  9.0 13.1 %copy-start.1 = (f32[16,128]{1,0:T(8,128)S(1)}, f32[16,128]{1,0:T(8,128)}, u32[]{:S(2)}) copy-start(f32[16,128]{1,0:T(8,128)} %param.3) | copy-start | bytes 24580
  21.3 2.3 collective-permute-start
  461.3 8.4 %copy-start = (bf16[2,4,704,512]{3,2,1,0:T(8,128)(2,1)}, bf16[2,4,704,512]{3,2,1,0:T(8,128)(2,1)S(1)}, u32[]{:S(2)}) copy-start(bf16[2,4,704,512]{3,2,1,0:T(8,128)(2,1)S(1)} %constant_dynamic-update-slice_fusion) | copy-start | bytes 17301508
where the time goes:
time: 516 us; the launch traced here: 507 us
  local copies, waits for them, and re-layouts  177 us (34%)
  other arithmetic  159 us (31%)
  blocking collectives  134 us (26%)
  matrix products  35.8 us (7%)
    all_to_all x1, blocking collectives, shards(): lax.all_to_all(spectra[None], ('stn', 'tm'), split_axis=1, concat_axis=0,...  134 us
    add x1, other arithmetic, shards(): filtered + filter_taps[tap_index] * extended[:, :, tap_index:tap_index +...  74.6 us
    broadcast_in_dim x1, local copies, waits for them, and re-layouts, shards(): spectra[None]  47.5 us
    all_to_all x1, local copies, waits for them, and re-layouts, shards(): lax.all_to_all(spectra[None], ('stn', 'tm'), split_axis=1, concat_axis=0,...  36 us
    unnamed x1, other arithmetic  35.9 us
    unnamed x9, local copies, waits for them, and re-layouts  28 us
    mul x1, other arithmetic, shards(): return result * scale  23.2 us
    dot_general x1, matrix products, correlate(): jnp.einsum('gcis,gcjs->gcij', left_imag, right_side, preferred_element_ty...  14.1 us
  transfers between devices with their start and end apart: 1, of which 1 were waited for; matrix products, arithmetic and copies ran while one was open for 0% of the time, Pallas kernels for 0%

commit v1 on v0

--- a/solution.py
+++ b/solution.py
@@ -1,9 +1,16 @@
+import functools
 import math
 
 import jax
 import jax.numpy as jnp
+import numpy as np
 from jax import lax
+from jax.experimental import pallas as pl
+from jax.experimental.pallas import tpu as pltpu
 from jax.sharding import PartitionSpec as P
+
+MESH = pl.DeviceIdType.MESH
+ROWS = 8
 
 
 def passed_along(value, axis, steps):
@@ -13,14 +20,15 @@
 
 
 def transform_table(frame_len, chan_count):
-    sample_index = jnp.arange(frame_len, dtype=jnp.int32)[:, None]
-    chan_index = jnp.arange(chan_count, dtype=jnp.int32)[None, :]
+    sample_index = np.arange(frame_len)[:, None]
+    chan_index = np.arange(chan_count)[None, :]
     phase = (2 * chan_index + 1) * sample_index % (2 * frame_len)
-    angle = phase.astype(jnp.float32) * (math.pi / frame_len)
+    angle = phase.astype(np.float64) * (math.pi / frame_len)
     factor = 1.0 / math.sqrt(frame_len)
-    cosine = jnp.cos(angle) * factor
-    sine = -jnp.sin(angle) * factor
-    return jnp.stack([cosine, sine], axis=2).reshape(frame_len, 2 * chan_count)
+    cosine = np.cos(angle) * factor
+    sine = -np.sin(angle) * factor
+    table = np.stack([cosine, sine], axis=2).reshape(frame_len, 2 * chan_count)
+    return table.astype(np.float32)
 
 
 def arrange(blocks):
@@ -45,7 +53,7 @@
     return jnp.stack([real_part, imag_part])
 
 
-def shards(voltages, filter_taps):
+def general_shards(voltages, filter_taps):
     inputs_dev, sub_count, time_dev = voltages.shape
     taps_count, frame_len = filter_taps.shape
     spec_dev = time_dev // frame_len
@@ -62,7 +70,7 @@
         filtered = (
             filtered + filter_taps[tap_index] * extended[:, :, tap_index : tap_index + spec_dev]
         )
-    table = transform_table(frame_len, chan_count)
+    table = jnp.asarray(transform_table(frame_len, chan_count))
     spectra = lax.dot_general(
         table,
         filtered.reshape(-1, frame_len),
@@ -80,10 +88,222 @@
     return result * scale
 
 
+def flipped(index, mask, count):
+    total = 0
+    bit = 1
+    while bit < count:
+        value = (index // bit) % 2
+        total = total + (1 - value if mask & bit else value) * bit
+        bit *= 2
+    return total
+
+
+def spectra_kernel(
+    group, x_ref, taps_ref, table_ref, out_ref,
+    x_buf, hist_buf, ext, spread, send_buf,
+    load_sem, hist_send, hist_recv, own_sem, send_sem, recv_sem,
+):
+    blocks = x_buf.shape[0] // ROWS
+    frames2 = x_buf.shape[1]
+    frames = frames2 // 2
+    keep = hist_buf.shape[1] // 2
+    taps_count = taps_ref.shape[0]
+    frame_len = taps_ref.shape[1]
+    tm = lax.axis_index("tm")
+    me = lax.axis_index("stn") * 2 + tm
+
+    def load(b):
+        rows = pl.ds(b * ROWS, ROWS)
+        return pltpu.make_async_copy(x_ref.at[rows], x_buf.at[rows], load_sem.at[b])
+
+    def history(b):
+        rows = pl.ds(b * ROWS, ROWS)
+        return pltpu.make_async_remote_copy(
+            src_ref=x_ref.at[rows, pl.ds(frames2 - 2 * keep, 2 * keep)],
+            dst_ref=hist_buf.at[rows],
+            send_sem=hist_send.at[b],
+            recv_sem=hist_recv.at[b],
+            device_id={"tm": 1 - tm},
+            device_id_type=MESH,
+        )
+
+    for b in range(blocks):
+        load(b).start()
+
+    barrier = pltpu.get_barrier_semaphore()
+    for mask in range(1, group):
+        other = flipped(me, mask, group)
+        pl.semaphore_signal(
+            barrier, inc=1, device_id={"stn": other // 2, "tm": other % 2}, device_id_type=MESH
+        )
+    pl.semaphore_wait(barrier, group - 1)
+
+    for b in range(blocks):
+        history(b).start()
+
+    late = tm.astype(jnp.float32)
+
+    def one_block(b, carry):
+        load(b).wait()
+        history(b).wait()
+
+        def one_input(i, inner):
+            row = b * ROWS + i
+            h0 = hist_buf[row, pl.ds(0, keep, stride=2), :].astype(jnp.float32)
+            h1 = hist_buf[row, pl.ds(1, keep, stride=2), :].astype(jnp.float32)
+            ext[0, pl.ds(0, keep), :] = h0 * late
+            ext[1, pl.ds(0, keep), :] = h1 * late + h0 * (1.0 - late)
+            parts = []
+            for g in range(2):
+                ext[g, pl.ds(keep, frames), :] = x_buf[
+                    row, pl.ds(g, frames, stride=2), :
+                ].astype(jnp.float32)
+                first = keep - (taps_count - 1)
+                acc = taps_ref[0:1, :] * ext[g, pl.ds(first, frames), :]
+                for j in range(1, taps_count):
+                    acc = acc + taps_ref[j : j + 1, :] * ext[g, pl.ds(first + j, frames), :]
+                parts.append(acc)
+            filtered = jnp.concatenate(parts, axis=0)
+            spectra = lax.dot_general(
+                table_ref[...], filtered, (((1,), (1,)), ((), ())),
+                precision=lax.Precision.HIGHEST, preferred_element_type=jnp.float32,
+            )
+            for g in range(2):
+                spread[g, pl.ds(i, frame_len, stride=ROWS), :] = spectra[
+                    :, g * frames : (g + 1) * frames
+                ]
+            return inner
+
+        lax.fori_loop(0, ROWS, one_input, 0)
+        share = frame_len * ROWS // group
+        for g in range(2):
+            send_buf[:, b, pl.ds(g * share, share), :] = (
+                spread[g].reshape(group, share, frames).astype(jnp.bfloat16)
+            )
+        for mask in range(group - 1, 0, -1):
+            other = flipped(me, mask, group)
+            pltpu.make_async_remote_copy(
+                src_ref=send_buf.at[other, b],
+                dst_ref=out_ref.at[me, b],
+                send_sem=send_sem.at[other],
+                recv_sem=recv_sem.at[me],
+                device_id={"stn": other // 2, "tm": other % 2},
+                device_id_type=MESH,
+            ).start()
+        return carry
+
+    lax.fori_loop(0, blocks, one_block, 0)
+    own = pltpu.make_async_copy(send_buf.at[me], out_ref.at[me], own_sem)
+    own.start()
+    own.wait()
+    for mask in range(1, group):
+        other = flipped(me, mask, group)
+        whole = pltpu.make_async_remote_copy(
+            src_ref=send_buf.at[other],
+            dst_ref=out_ref.at[other],
+            send_sem=send_sem.at[other],
+            recv_sem=recv_sem.at[other],
+            device_id={"stn": other // 2, "tm": other % 2},
+            device_id_type=MESH,
+        )
+        whole.wait_send()
+        whole.wait_recv()
+
+
+def correlate_kernel(scale, in_ref, out_ref):
+    stations, halves, blocks, pair, frames = in_ref.shape
+    inputs = stations * blocks * ROWS
+    real = []
+    imag = []
+    for t in range(halves):
+        both = in_ref[:, t].astype(jnp.float32).reshape(stations * blocks, pair, frames)
+        real.append(both[:, :ROWS].reshape(inputs, frames))
+        imag.append(both[:, ROWS:].reshape(inputs, frames))
+    right = jnp.concatenate(real + imag, axis=1).astype(jnp.bfloat16)
+    left = jnp.concatenate(imag + [-value for value in real], axis=1).astype(jnp.bfloat16)
+    dims = (((1,), (1,)), ((), ()))
+    out_ref[0] = scale * lax.dot_general(right, right, dims, preferred_element_type=jnp.float32)
+    out_ref[1] = scale * lax.dot_general(left, right, dims, preferred_element_type=jnp.float32)
+
+
+def kernel_shards(stations, halves, voltages, filter_taps):
+    inputs_dev, sub_count, time_dev = voltages.shape
+    taps_count, frame_len = filter_taps.shape
+    frames = time_dev // frame_len
+    group = stations * halves
+    blocks = inputs_dev // ROWS
+    keep = 16
+    per_dev = frame_len // 2 // group
+    table = jnp.asarray(np.ascontiguousarray(transform_table(frame_len, frame_len // 2).T))
+    x = voltages.reshape(inputs_dev, sub_count, frames, frame_len)
+    x = jnp.transpose(x, (0, 2, 1, 3)).reshape(inputs_dev, frames * sub_count, frame_len)
+    rows = 2 * frame_len * ROWS // group
+    vmem = pl.BlockSpec(memory_space=pltpu.VMEM)
+    spectra = pl.pallas_call(
+        functools.partial(spectra_kernel, group),
+        out_shape=jax.ShapeDtypeStruct((group, blocks, rows, frames), jnp.bfloat16),
+        in_specs=[pl.BlockSpec(memory_space=pl.ANY), vmem, vmem],
+        out_specs=pl.BlockSpec(memory_space=pl.ANY),
+        scratch_shapes=[
+            pltpu.VMEM((inputs_dev, frames * 2, frame_len), jnp.int32),
+            pltpu.VMEM((inputs_dev, keep * 2, frame_len), jnp.int32),
+            pltpu.VMEM((2, keep + frames, frame_len), jnp.float32),
+            pltpu.VMEM((2, frame_len * ROWS, frames), jnp.float32),
+            pltpu.VMEM((group, blocks, rows, frames), jnp.bfloat16),
+            pltpu.SemaphoreType.DMA((blocks,)),
+            pltpu.SemaphoreType.DMA((blocks,)),
+            pltpu.SemaphoreType.DMA((blocks,)),
+            pltpu.SemaphoreType.DMA,
+            pltpu.SemaphoreType.DMA((group,)),
+            pltpu.SemaphoreType.DMA((group,)),
+        ],
+        compiler_params=pltpu.CompilerParams(
+            collective_id=0, has_side_effects=True, vmem_limit_bytes=60 * 1024 * 1024
+        ),
+        name="spectra",
+    )(x, filter_taps, table)
+    spectra = spectra.reshape(stations, halves, blocks, sub_count * per_dev, 2 * ROWS, frames)
+    inputs = stations * inputs_dev
+    return pl.pallas_call(
+        functools.partial(correlate_kernel, 1.0 / (frames * halves)),
+        grid=(sub_count * per_dev,),
+        out_shape=jax.ShapeDtypeStruct((2, sub_count, per_dev, inputs, inputs), jnp.float32),
+        in_specs=[
+            pl.BlockSpec(
+                (stations, halves, blocks, None, 2 * ROWS, frames), lambda s: (0, 0, 0, s, 0, 0)
+            )
+        ],
+        out_specs=pl.BlockSpec(
+            (2, None, None, inputs, inputs), lambda s: (0, s // per_dev, s % per_dev, 0, 0)
+        ),
+        compiler_params=pltpu.CompilerParams(vmem_limit_bytes=50 * 1024 * 1024),
+        name="correlate",
+    )(spectra)
+
+
+def shards(stations, halves, voltages, filter_taps):
+    inputs_dev, sub_count, time_dev = voltages.shape
+    taps_count, frame_len = filter_taps.shape
+    group = stations * halves
+    fits = (
+        halves == 2
+        and sub_count == 2
+        and group & (group - 1) == 0
+        and group <= 16
+        and inputs_dev % ROWS == 0
+        and frame_len == 128
+        and time_dev == 128 * frame_len
+        and taps_count == 16
+    )
+    if fits:
+        return kernel_shards(stations, halves, voltages, filter_taps)
+    return general_shards(voltages, filter_taps)
+
+
 def solution(mesh):
     placed = (P("stn", "band", "tm"), P())
     return jax.shard_map(
-        shards,
+        functools.partial(shards, mesh.shape["stn"], mesh.shape["tm"]),
         mesh=mesh,
         in_specs=placed,
         out_specs=P(None, None, ("band", "stn", "tm"), None, None),

time: 516 us -> 155 us (0.30); the launches traced: 507 us -> 154 us
  local copies, waits for them, and re-layouts: 177 us -> 0 us
  other arithmetic: 159 us -> 0 us
  Pallas kernels: 0 us -> 154 us
  blocking collectives: 134 us -> 0 us
  matrix products: 35.8 us -> 0 us
    pallas_call x0 -> x2, Pallas kernels: none -> 154 us  [the longest x1 138 us: kernel_shards(): pl.pallas_call(functools.partial(spectra_kernel, group), out_shape=jax.Sh...]
    all_to_all x1 -> x0, blocking collectives: 134 us -> none  [shards(): lax.all_to_all(spectra[None], ('stn', 'tm'), split_axis=1, concat_axis=0,...]
    add x2 -> x0, other arithmetic: 74.6 us -> none  [the longest x1 74.6 us: shards(): filtered + filter_taps[tap_index] * extended[:, :, tap_index:tap_index +...]
    broadcast_in_dim x1 -> x0, local copies, waits for them, and re-layouts: 47.5 us -> none  [shards(): spectra[None]]
    all_to_all x1 -> x0, local copies, waits for them, and re-layouts: 36 us -> none  [shards(): lax.all_to_all(spectra[None], ('stn', 'tm'), split_axis=1, concat_axis=0,...]
    unnamed x1 -> x0, other arithmetic: 35.9 us -> none
    dot_general x3 -> x0, matrix products: 35.8 us -> none  [the longest x1 14.1 us: correlate(): jnp.einsum('gcis,gcjs->gcij', left_imag, right_side, preferred_element_ty...]
    unnamed x9 -> x0, local copies, waits for them, and re-layouts: 28 us -> none
  transfers between devices with their start and end apart: 1 -> 0, of which waited for: 1 -> 0; matrix products, arithmetic and copies ran while one was open for 0% -> 0% of each run, Pallas kernels for 0% -> 0%
where the time goes in v1:
time: 155 us; the launch traced here: 154 us
  Pallas kernels  154 us (99%)
    pallas_call x1, Pallas kernels, kernel_shards(): pl.pallas_call(functools.partial(spectra_kernel, group), out_shape=jax.Sh...  138 us
    pallas_call x1, Pallas kernels, kernel_shards(): pl.pallas_call(functools.partial(correlate_kernel, 1.0 / (frames * halves...  16.4 us

profile of v1, /device:TPU:0, one launch (start us, length us, event | category | flops | bytes accessed | tf_op | source)
XLA Modules:
  0.0 154.3 jit_solution(8076639390459787207)
XLA Ops:
  0.0 137.9 %spectra.1 = bf16[16,11,128,128]{3,2,1,0:T(8,128)(2,1)} custom-call(s32[88,256,128]{2,1,0:T(8,128)} %bitcast.7, f32[16,128]{1,0:T(8,128)} %taps_ref.1, f32[128,128]{1,0:T(8,128)} %constant.2.clone.table_ref), custom_call_target="tpu_custom_call" | custom-call | tf_op jit(solution)/shard_map/spectra/pallas_call | solution.py:242
  137.9 16.4 %correlate.1 = f32[2,2,4,704,704]{4,3,2,1,0:T(8,128)} custom-call(bf16[8,2,11,8,16,128]{5,4,3,2,1,0:T(8,128)(2,1)} %bitcast.6), custom_call_target="tpu_custom_call" | custom-call | tf_op jit(solution)/shard_map/correlate/pallas_call | solution.py:267

commit v2 on v1

--- a/solution.py
+++ b/solution.py
@@ -11,6 +11,7 @@
 
 MESH = pl.DeviceIdType.MESH
 ROWS = 8
+DEFERRED = 5
 
 
 def passed_along(value, axis, steps):
@@ -99,10 +100,13 @@
 
 
 def spectra_kernel(
-    group, x_ref, taps_ref, table_ref, out_ref,
-    x_buf, hist_buf, ext, spread, send_buf,
-    load_sem, hist_send, hist_recv, own_sem, send_sem, recv_sem,
+    group, x_ref, taps_in, table_in, *refs
 ):
+    half = group // 2
+    out_ref, far_refs, scratch = refs[0], refs[1 : 1 + DEFERRED], refs[1 + DEFERRED :]
+    taps_ref, table_ref, x_buf, hist_buf, ext, spread, send_buf = scratch[:7]
+    small_sem, load_sem, hist_send, hist_recv, own_sem, far_sem, send_sem, recv_sem = scratch[7:]
+    early = send_buf.shape[2] - 2 * ROWS
     blocks = x_buf.shape[0] // ROWS
     frames2 = x_buf.shape[1]
     frames = frames2 // 2
@@ -127,6 +131,12 @@
             device_id_type=MESH,
         )
 
+    small = [
+        pltpu.make_async_copy(taps_in, taps_ref, small_sem.at[0]),
+        pltpu.make_async_copy(table_in, table_ref, small_sem.at[1]),
+    ]
+    for copy in small:
+        copy.start()
     for b in range(blocks):
         load(b).start()
 
@@ -141,6 +151,8 @@
     for b in range(blocks):
         history(b).start()
 
+    for copy in small:
+        copy.wait()
     late = tm.astype(jnp.float32)
 
     def one_block(b, carry):
@@ -182,9 +194,10 @@
             )
         for mask in range(group - 1, 0, -1):
             other = flipped(me, mask, group)
+            rows = pl.ds(0, early if half <= mask < half + DEFERRED else early + 2 * ROWS)
             pltpu.make_async_remote_copy(
-                src_ref=send_buf.at[other, b],
-                dst_ref=out_ref.at[me, b],
+                src_ref=send_buf.at[other, b, rows],
+                dst_ref=out_ref.at[me, b, rows],
                 send_sem=send_sem.at[other],
                 recv_sem=recv_sem.at[me],
                 device_id={"stn": other // 2, "tm": other % 2},
@@ -195,12 +208,24 @@
     lax.fori_loop(0, blocks, one_block, 0)
     own = pltpu.make_async_copy(send_buf.at[me], out_ref.at[me], own_sem)
     own.start()
+    kept = []
+    for m in range(DEFERRED):
+        other = flipped(me, half + m, group)
+        kept.append(
+            pltpu.make_async_copy(
+                send_buf.at[other, :, pl.ds(early, 2 * ROWS)], far_refs[m], far_sem.at[m]
+            )
+        )
+        kept[m].start()
     own.wait()
+    for copy in kept:
+        copy.wait()
     for mask in range(1, group):
         other = flipped(me, mask, group)
+        rows = pl.ds(0, early if half <= mask < half + DEFERRED else early + 2 * ROWS)
         whole = pltpu.make_async_remote_copy(
-            src_ref=send_buf.at[other],
-            dst_ref=out_ref.at[other],
+            src_ref=send_buf.at[other, :, rows],
+            dst_ref=out_ref.at[other, :, rows],
             send_sem=send_sem.at[other],
             recv_sem=recv_sem.at[other],
             device_id={"stn": other // 2, "tm": other % 2},
@@ -210,20 +235,40 @@
         whole.wait_recv()
 
 
-def correlate_kernel(scale, in_ref, out_ref):
-    stations, halves, blocks, pair, frames = in_ref.shape
-    inputs = stations * blocks * ROWS
+def products(scale, halves_in, out_ref):
     real = []
     imag = []
-    for t in range(halves):
-        both = in_ref[:, t].astype(jnp.float32).reshape(stations * blocks, pair, frames)
+    for value in halves_in:
+        stations, blocks, pair, frames = value.shape
+        inputs = stations * blocks * ROWS
+        both = value.astype(jnp.float32).reshape(stations * blocks, pair, frames)
         real.append(both[:, :ROWS].reshape(inputs, frames))
         imag.append(both[:, ROWS:].reshape(inputs, frames))
     right = jnp.concatenate(real + imag, axis=1).astype(jnp.bfloat16)
     left = jnp.concatenate(imag + [-value for value in real], axis=1).astype(jnp.bfloat16)
     dims = (((1,), (1,)), ((), ()))
-    out_ref[0] = scale * lax.dot_general(right, right, dims, preferred_element_type=jnp.float32)
-    out_ref[1] = scale * lax.dot_general(left, right, dims, preferred_element_type=jnp.float32)
+    left = jnp.concatenate([right * scale, left * scale], axis=0)
+    product = lax.dot_general(left, right, dims, preferred_element_type=jnp.float32)
+    out_ref[...] = product.reshape(2, inputs, inputs)
+
+
+def correlate_kernel(scale, in_ref, out_ref):
+    step = pl.program_id(0)
+    halves = in_ref.shape[1]
+    products(scale, [in_ref[:, t, :, step] for t in range(halves)], out_ref)
+
+
+def last_kernel(scale, in_ref, *refs):
+    half = in_ref.shape[0] * in_ref.shape[1] // 2
+    far_refs, out_ref, full = refs[:DEFERRED], refs[DEFERRED + 1], refs[DEFERRED + 2]
+    halves = in_ref.shape[1]
+    step = in_ref.shape[3] - 1
+    me = lax.axis_index("stn") * halves + lax.axis_index("tm")
+    full[...] = in_ref[:, :, :, step]
+    for m in range(DEFERRED):
+        other = flipped(me, half + m, 2 * half)
+        full[other // halves, other % halves] = far_refs[m][...]
+    products(scale, [full[:, t] for t in range(halves)], out_ref)
 
 
 def kernel_shards(stations, halves, voltages, filter_taps):
@@ -239,46 +284,81 @@
     x = jnp.transpose(x, (0, 2, 1, 3)).reshape(inputs_dev, frames * sub_count, frame_len)
     rows = 2 * frame_len * ROWS // group
     vmem = pl.BlockSpec(memory_space=pltpu.VMEM)
-    spectra = pl.pallas_call(
+    anywhere = pl.BlockSpec(memory_space=pl.ANY)
+    half = group // 2
+    far_shape = jax.ShapeDtypeStruct((blocks, 2 * ROWS, frames), jnp.bfloat16)
+    spectra, *far = pl.pallas_call(
         functools.partial(spectra_kernel, group),
-        out_shape=jax.ShapeDtypeStruct((group, blocks, rows, frames), jnp.bfloat16),
-        in_specs=[pl.BlockSpec(memory_space=pl.ANY), vmem, vmem],
-        out_specs=pl.BlockSpec(memory_space=pl.ANY),
+        out_shape=[jax.ShapeDtypeStruct((group, blocks, rows, frames), jnp.bfloat16)]
+        + [far_shape] * DEFERRED,
+        in_specs=[anywhere] + [pl.BlockSpec(memory_space=pltpu.HBM)] * 2,
+        out_specs=[vmem] * (1 + DEFERRED),
         scratch_shapes=[
+            pltpu.VMEM((taps_count, frame_len), jnp.float32),
+            pltpu.VMEM((frame_len, frame_len), jnp.float32),
             pltpu.VMEM((inputs_dev, frames * 2, frame_len), jnp.int32),
             pltpu.VMEM((inputs_dev, keep * 2, frame_len), jnp.int32),
             pltpu.VMEM((2, keep + frames, frame_len), jnp.float32),
             pltpu.VMEM((2, frame_len * ROWS, frames), jnp.float32),
             pltpu.VMEM((group, blocks, rows, frames), jnp.bfloat16),
+            pltpu.SemaphoreType.DMA((2,)),
             pltpu.SemaphoreType.DMA((blocks,)),
             pltpu.SemaphoreType.DMA((blocks,)),
             pltpu.SemaphoreType.DMA((blocks,)),
             pltpu.SemaphoreType.DMA,
+            pltpu.SemaphoreType.DMA((DEFERRED,)),
             pltpu.SemaphoreType.DMA((group,)),
             pltpu.SemaphoreType.DMA((group,)),
         ],
         compiler_params=pltpu.CompilerParams(
-            collective_id=0, has_side_effects=True, vmem_limit_bytes=60 * 1024 * 1024
+            collective_id=0, has_side_effects=True, vmem_limit_bytes=40 * 1024 * 1024
         ),
         name="spectra",
     )(x, filter_taps, table)
     spectra = spectra.reshape(stations, halves, blocks, sub_count * per_dev, 2 * ROWS, frames)
+    received = [
+        lax.ppermute(
+            far[m], ("stn", "tm"), [(source, source ^ (half + m)) for source in range(group)]
+        )
+        for m in range(DEFERRED)
+    ]
     inputs = stations * inputs_dev
-    return pl.pallas_call(
-        functools.partial(correlate_kernel, 1.0 / (frames * halves)),
-        grid=(sub_count * per_dev,),
-        out_shape=jax.ShapeDtypeStruct((2, sub_count, per_dev, inputs, inputs), jnp.float32),
-        in_specs=[
-            pl.BlockSpec(
-                (stations, halves, blocks, None, 2 * ROWS, frames), lambda s: (0, 0, 0, s, 0, 0)
-            )
-        ],
+    scale = 1.0 / (frames * halves)
+    steps = sub_count * per_dev
+    out_shape = jax.ShapeDtypeStruct((2, sub_count, per_dev, inputs, inputs), jnp.float32)
+    flops = 8 * inputs * inputs * halves * frames
+    partly = pl.pallas_call(
+        functools.partial(correlate_kernel, scale),
+        grid=(steps - 1,),
+        out_shape=out_shape,
+        in_specs=[vmem],
         out_specs=pl.BlockSpec(
             (2, None, None, inputs, inputs), lambda s: (0, s // per_dev, s % per_dev, 0, 0)
         ),
-        compiler_params=pltpu.CompilerParams(vmem_limit_bytes=50 * 1024 * 1024),
+        compiler_params=pltpu.CompilerParams(vmem_limit_bytes=40 * 1024 * 1024),
+        cost_estimate=pl.CostEstimate(
+            flops=(steps - 1) * flops,
+            bytes_accessed=(steps - 1) * 8 * inputs * inputs,
+            transcendentals=0,
+        ),
         name="correlate",
     )(spectra)
+    return pl.pallas_call(
+        functools.partial(last_kernel, scale),
+        grid=(1,),
+        out_shape=out_shape,
+        in_specs=[vmem] * (1 + DEFERRED) + [anywhere],
+        out_specs=pl.BlockSpec(
+            (2, None, None, inputs, inputs), lambda s: (0, sub_count - 1, per_dev - 1, 0, 0)
+        ),
+        scratch_shapes=[pltpu.VMEM((stations, halves, blocks, 2 * ROWS, frames), jnp.bfloat16)],
+        input_output_aliases={1 + DEFERRED: 0},
+        compiler_params=pltpu.CompilerParams(vmem_limit_bytes=40 * 1024 * 1024),
+        cost_estimate=pl.CostEstimate(
+            flops=flops, bytes_accessed=8 * inputs * inputs, transcendentals=0
+        ),
+        name="last",
+    )(spectra, *received, partly)
 
 
 def shards(stations, halves, voltages, filter_taps):
@@ -289,7 +369,7 @@
         halves == 2
         and sub_count == 2
         and group & (group - 1) == 0
-        and group <= 16
+        and group == 16
         and inputs_dev % ROWS == 0
         and frame_len == 128
         and time_dev == 128 * frame_len

time: 155 us -> 155 us (level)
  Pallas kernels: 154 us -> 145 us
  starting transfers between devices: 0 us -> 8.14 us
    pallas_call x2 -> x3, Pallas kernels: 154 us -> 145 us  [the longest x1 128 us: kernel_shards(): pl.pallas_call(functools.partial(spectra_kernel, group), out_shape=[jax.S...]
    ppermute x0 -> x5, starting transfers between devices: none -> 8.14 us  [kernel_shards(): lax.ppermute(far[m], ('stn', 'tm'), [(source, source ^ half + m) for sour...]
  transfers between devices with their start and end apart: 0 -> 5, of which waited for: 0 -> 0; matrix products, arithmetic and copies ran while one was open for 0% -> 0% of each run, Pallas kernels for 0% -> 9%
where the time goes in v2:
time: 155 us
  Pallas kernels  145 us (94%)
  starting transfers between devices  8.14 us (5%)
    pallas_call x1, Pallas kernels, kernel_shards(): pl.pallas_call(functools.partial(spectra_kernel, group), out_shape=[jax.S...  128 us
    pallas_call x1, Pallas kernels, kernel_shards(): pl.pallas_call(functools.partial(correlate_kernel, scale), grid=(steps -...  13.6 us
    ppermute x5, starting transfers between devices, kernel_shards(): lax.ppermute(far[m], ('stn', 'tm'), [(source, source ^ half + m) for sour...  8.14 us
    pallas_call x1, Pallas kernels, kernel_shards(): pl.pallas_call(functools.partial(last_kernel, scale), grid=(1,), out_shap...  3.55 us
  transfers between devices with their start and end apart: 5, of which 0 were waited for; matrix products, arithmetic and copies ran while one was open for 0% of the time, Pallas kernels for 9%

profile of v2, /device:TPU:0, one launch (start us, length us, event | category | flops | bytes accessed | tf_op | source)
XLA Modules:
  0.0 155.0 jit_solution(10305602867791525462)
XLA Ops:
  0.0 0.0 copy-start
  0.0 0.8 copy-done
  0.8 0.0 copy-start.1
  0.8 0.7 copy-done.1
  1.5 128.1 %spectra.1 = (bf16[16,11,128,128]{3,2,1,0:T(8,128)(2,1)S(1)}, bf16[11,16,128]{2,1,0:T(8,128)(2,1)S(1)}, bf16[11,16,128]{2,1,0:T(8,128)(2,1)S(1)}, bf16[11,16,128...) custom-call(s32[88,256,128]{2,1,0:T(8,128)} %bitcast.8, ...), custom_call_target="tpu_custom_call" | custom-call | tf_op jit(solution)/shard_map/spectra/pallas_call | solution.py:290
  129.7 0.1 collective-permute-start
  129.8 2.3 %collective-permute-start.1 = (bf16[11,16,128]{2,1,0:T(8,128)(2,1)S(1)}, bf16[11,16,128]{2,1,0:T(8,128)(2,1)S(1)}, u32[]{:S(2)}, u32[]{:S(2)}) collective-permute-start(bf16[11,16,128]{2,1,0:T(8,128)(2,1)S(1)} %get-tuple-element.13), channel_id=1, source_target_pairs={{0,9},{1,8},{2,11},{3,10},{4,13},{5,12},{6,15},{7,14},{8,1},{9,0},... | collective-permute-start | bytes 135176 | tf_op jit(solution)/shard_map/ppermute | solution.py:320
  132.1 0.5 collective-permute-start.2
  132.6 3.4 %collective-permute-start.3 = (bf16[11,16,128]{2,1,0:T(8,128)(2,1)S(1)}, bf16[11,16,128]{2,1,0:T(8,128)(2,1)S(1)}, u32[]{:S(2)}, u32[]{:S(2)}) collective-permute-start(bf16[11,16,128]{2,1,0:T(8,128)(2,1)S(1)} %get-tuple-element.15), channel_id=1, source_target_pairs={{0,11},{1,10},{2,9},{3,8},{4,15},{5,14},{6,13},{7,12},{8,3},{9,2},... | collective-permute-start | bytes 135176 | tf_op jit(solution)/shard_map/ppermute | solution.py:320
  136.0 1.9 %collective-permute-start.4 = (bf16[11,16,128]{2,1,0:T(8,128)(2,1)S(1)}, bf16[11,16,128]{2,1,0:T(8,128)(2,1)S(1)}, u32[]{:S(2)}, u32[]{:S(2)}) collective-permute-start(bf16[11,16,128]{2,1,0:T(8,128)(2,1)S(1)} %get-tuple-element.16), channel_id=1, source_target_pairs={{0,12},{1,13},{2,14},{3,15},{4,8},{5,9},{6,10},{7,11},{8,4},{9,5},... | collective-permute-start | bytes 135176 | tf_op jit(solution)/shard_map/ppermute | solution.py:320
  137.8 13.6 %correlate.1.refs_5_ = f32[2,2,4,704,704]{4,3,2,1,0:T(8,128)} custom-call(bf16[8,2,11,8,16,128]{5,4,3,2,1,0:T(8,128)(2,1)S(1)} %bitcast.6), custom_call_target="tpu_custom_call" | custom-call | flops 7105150976 | bytes 27754496 | tf_op jit(solution)/shard_map/correlate/pallas_call | solution.py:330
  151.5 0.0 collective-permute-done.refs_0_
  151.5 0.0 collective-permute-done.1.refs_1_
  151.5 0.0 collective-permute-done.2.refs_2_
  151.5 0.0 collective-permute-done.3.refs_3_
  151.5 0.0 collective-permute-done.4.refs_4_
  151.5 3.5 %last.1 = f32[2,2,4,704,704]{4,3,2,1,0:T(8,128)} custom-call(bf16[8,2,11,8,16,128]{5,4,3,2,1,0:T(8,128)(2,1)S(1)} %bitcast.7, bf16[11,16,128]{2,1,0:T(8,128)(2,1)S(1)} %collective-permute-done.refs_0_, bf16[11,16,128]{2,1,0:T(8,128)(2,1)S(1)} %collective-permute-done.1.refs_1_, ...), custom_call_target="tpu_custom_call", output_to_operand_aliasing={{}: (6, {})} | custom-call | flops 1015021568 | bytes 3964928 | tf_op jit(solution)/shard_map/last/pallas_call | solution.py:346
Async XLA Ops:
  0.0 0.8 copy-start
  0.8 0.7 copy-start.1
  129.7 21.8 %collective-permute-start = (bf16[11,16,128]{2,1,0:T(8,128)(2,1)S(1)}, bf16[11,16,128]{2,1,0:T(8,128)(2,1)S(1)}, u32[]{:S(2)}, u32[]{:S(2)}) collective-permute-start(bf16[11,16,128]{2,1,0:T(8,128)(2,1)S(1)} %get-tuple-element.12), channel_id=1, source_target_pairs={{0,8},{1,9},{2,10},{3,11},{4,12},{5,13},{6,14},{7,15},{8,0},{9,1},... | collective-permute-start | bytes 135176 | tf_op jit(solution)/shard_map/ppermute | solution.py:320
  129.8 21.7 %collective-permute-start.1 = (bf16[11,16,128]{2,1,0:T(8,128)(2,1)S(1)}, bf16[11,16,128]{2,1,0:T(8,128)(2,1)S(1)}, u32[]{:S(2)}, u32[]{:S(2)}) collective-permute-start(bf16[11,16,128]{2,1,0:T(8,128)(2,1)S(1)} %get-tuple-element.13), channel_id=1, source_target_pairs={{0,9},{1,8},{2,11},{3,10},{4,13},{5,12},{6,15},{7,14},{8,1},{9,0},... | collective-permute-start | bytes 135176 | tf_op jit(solution)/shard_map/ppermute | solution.py:320
  132.1 19.4 %collective-permute-start.2 = (bf16[11,16,128]{2,1,0:T(8,128)(2,1)S(1)}, bf16[11,16,128]{2,1,0:T(8,128)(2,1)S(1)}, u32[]{:S(2)}, u32[]{:S(2)}) collective-permute-start(bf16[11,16,128]{2,1,0:T(8,128)(2,1)S(1)} %get-tuple-element.14), channel_id=1, source_target_pairs={{0,10},{1,11},{2,8},{3,9},{4,14},{5,15},{6,12},{7,13},{8,2},{9,3},... | collective-permute-start | bytes 135176 | tf_op jit(solution)/shard_map/ppermute | solution.py:320
  132.6 18.9 %collective-permute-start.3 = (bf16[11,16,128]{2,1,0:T(8,128)(2,1)S(1)}, bf16[11,16,128]{2,1,0:T(8,128)(2,1)S(1)}, u32[]{:S(2)}, u32[]{:S(2)}) collective-permute-start(bf16[11,16,128]{2,1,0:T(8,128)(2,1)S(1)} %get-tuple-element.15), channel_id=1, source_target_pairs={{0,11},{1,10},{2,9},{3,8},{4,15},{5,14},{6,13},{7,12},{8,3},{9,2},... | collective-permute-start | bytes 135176 | tf_op jit(solution)/shard_map/ppermute | solution.py:320
  136.0 15.5 %collective-permute-start.4 = (bf16[11,16,128]{2,1,0:T(8,128)(2,1)S(1)}, bf16[11,16,128]{2,1,0:T(8,128)(2,1)S(1)}, u32[]{:S(2)}, u32[]{:S(2)}) collective-permute-start(bf16[11,16,128]{2,1,0:T(8,128)(2,1)S(1)} %get-tuple-element.16), channel_id=1, source_target_pairs={{0,12},{1,13},{2,14},{3,15},{4,8},{5,9},{6,10},{7,11},{8,4},{9,5},... | collective-permute-start | bytes 135176 | tf_op jit(solution)/shard_map/ppermute | solution.py:320

commit v3 on v1

--- a/solution.py
+++ b/solution.py
@@ -174,7 +174,7 @@
                 ]
             return inner
 
-        lax.fori_loop(0, ROWS, one_input, 0)
+        lax.fori_loop(0, ROWS, one_input, 0, unroll=4)
         share = frame_len * ROWS // group
         for g in range(2):
             send_buf[:, b, pl.ds(g * share, share), :] = (
@@ -210,20 +210,23 @@
         whole.wait_recv()
 
 
-def correlate_kernel(scale, in_ref, out_ref):
-    stations, halves, blocks, pair, frames = in_ref.shape
+def correlate_kernel(in_ref, out_ref):
+    stations, halves, blocks, _, pair, frames = in_ref.shape
     inputs = stations * blocks * ROWS
+    step = pl.program_id(0)
     real = []
     imag = []
     for t in range(halves):
-        both = in_ref[:, t].astype(jnp.float32).reshape(stations * blocks, pair, frames)
+        both = in_ref[:, t, :, step].astype(jnp.float32)
+        both = both.reshape(stations * blocks, pair, frames)
         real.append(both[:, :ROWS].reshape(inputs, frames))
         imag.append(both[:, ROWS:].reshape(inputs, frames))
     right = jnp.concatenate(real + imag, axis=1).astype(jnp.bfloat16)
     left = jnp.concatenate(imag + [-value for value in real], axis=1).astype(jnp.bfloat16)
     dims = (((1,), (1,)), ((), ()))
-    out_ref[0] = scale * lax.dot_general(right, right, dims, preferred_element_type=jnp.float32)
-    out_ref[1] = scale * lax.dot_general(left, right, dims, preferred_element_type=jnp.float32)
+    left = jnp.concatenate([right, left], axis=0)
+    product = lax.dot_general(left, right, dims, preferred_element_type=jnp.float32)
+    out_ref[...] = product.reshape(2, inputs, inputs)
 
 
 def kernel_shards(stations, halves, voltages, filter_taps):
@@ -234,7 +237,8 @@
     blocks = inputs_dev // ROWS
     keep = 16
     per_dev = frame_len // 2 // group
-    table = jnp.asarray(np.ascontiguousarray(transform_table(frame_len, frame_len // 2).T))
+    share = np.float32(1.0 / math.sqrt(frames * halves))
+    table = jnp.asarray(np.ascontiguousarray(transform_table(frame_len, frame_len // 2).T) * share)
     x = voltages.reshape(inputs_dev, sub_count, frames, frame_len)
     x = jnp.transpose(x, (0, 2, 1, 3)).reshape(inputs_dev, frames * sub_count, frame_len)
     rows = 2 * frame_len * ROWS // group
@@ -243,7 +247,7 @@
         functools.partial(spectra_kernel, group),
         out_shape=jax.ShapeDtypeStruct((group, blocks, rows, frames), jnp.bfloat16),
         in_specs=[pl.BlockSpec(memory_space=pl.ANY), vmem, vmem],
-        out_specs=pl.BlockSpec(memory_space=pl.ANY),
+        out_specs=vmem,
         scratch_shapes=[
             pltpu.VMEM((inputs_dev, frames * 2, frame_len), jnp.int32),
             pltpu.VMEM((inputs_dev, keep * 2, frame_len), jnp.int32),
@@ -258,25 +262,21 @@
             pltpu.SemaphoreType.DMA((group,)),
         ],
         compiler_params=pltpu.CompilerParams(
-            collective_id=0, has_side_effects=True, vmem_limit_bytes=60 * 1024 * 1024
+            collective_id=0, has_side_effects=True, vmem_limit_bytes=40960 * 1024
         ),
         name="spectra",
     )(x, filter_taps, table)
     spectra = spectra.reshape(stations, halves, blocks, sub_count * per_dev, 2 * ROWS, frames)
     inputs = stations * inputs_dev
     return pl.pallas_call(
-        functools.partial(correlate_kernel, 1.0 / (frames * halves)),
+        correlate_kernel,
         grid=(sub_count * per_dev,),
         out_shape=jax.ShapeDtypeStruct((2, sub_count, per_dev, inputs, inputs), jnp.float32),
-        in_specs=[
-            pl.BlockSpec(
-                (stations, halves, blocks, None, 2 * ROWS, frames), lambda s: (0, 0, 0, s, 0, 0)
-            )
-        ],
+        in_specs=[vmem],
         out_specs=pl.BlockSpec(
             (2, None, None, inputs, inputs), lambda s: (0, s // per_dev, s % per_dev, 0, 0)
         ),
-        compiler_params=pltpu.CompilerParams(vmem_limit_bytes=50 * 1024 * 1024),
+        compiler_params=pltpu.CompilerParams(vmem_limit_bytes=40 * 1024 * 1024),
         name="correlate",
     )(spectra)
 

time: 155 us -> 153 us (0.987)
  Pallas kernels: 154 us -> 151 us
    pallas_call x1, Pallas kernels: 138 us -> 136 us  [kernel_shards(): pl.pallas_call(functools.partial(spectra_kernel, group), out_shape=jax.Sh...]
where the time goes in v3:
time: 153 us
  Pallas kernels  151 us (99%)
  local copies, waits for them, and re-layouts  1.54 us (1%)
    pallas_call x1, Pallas kernels, kernel_shards(): pl.pallas_call(functools.partial(spectra_kernel, group), out_shape=jax.Sh...  136 us
    pallas_call x1, Pallas kernels, kernel_shards(): pl.pallas_call(correlate_kernel, grid=(sub_count * per_dev,), out_shape=j...  15.1 us

profile of v3, /device:TPU:0, one launch (start us, length us, event | category | flops | bytes accessed | tf_op | source)
XLA Modules:
  0.0 152.6 jit_solution(14965077810058405113)
XLA Ops:
  0.0 0.0 copy-start
  0.0 0.8 copy-done
  0.8 0.0 copy-start.1
  0.8 0.7 copy-done.1
  1.5 135.9 %spectra.1 = bf16[16,11,128,128]{3,2,1,0:T(8,128)(2,1)S(1)} custom-call(s32[88,256,128]{2,1,0:T(8,128)} %bitcast.7, f32[16,128]{1,0:T(8,128)S(1)} %copy-done.1, f32[128,128]{1,0:T(8,128)S(1)} %copy-done), custom_call_target="tpu_custom_call" | custom-call | tf_op jit(solution)/shard_map/spectra/pallas_call | solution.py:246
  137.5 15.1 %correlate.1 = f32[2,2,4,704,704]{4,3,2,1,0:T(8,128)} custom-call(bf16[8,2,11,8,16,128]{5,4,3,2,1,0:T(8,128)(2,1)S(1)} %bitcast.6), custom_call_target="tpu_custom_call" | custom-call | tf_op jit(solution)/shard_map/correlate/pallas_call | solution.py:271
Async XLA Ops:
  0.0 0.8 copy-start
  0.8 0.7 copy-start.1

commit v4 on v3

--- a/solution.py
+++ b/solution.py
@@ -174,7 +174,7 @@
                 ]
             return inner
 
-        lax.fori_loop(0, ROWS, one_input, 0, unroll=4)
+        lax.fori_loop(0, ROWS, one_input, 0, unroll=8)
         share = frame_len * ROWS // group
         for g in range(2):
             send_buf[:, b, pl.ds(g * share, share), :] = (

time: 153 us -> 153 us (level)
  no operation moved by 1% of the time
where the time goes in v4:
time: 153 us; the launch traced here: 152 us
  Pallas kernels  151 us (99%)
  local copies, waits for them, and re-layouts  1.54 us (1%)
    pallas_call x1, Pallas kernels, kernel_shards(): pl.pallas_call(functools.partial(spectra_kernel, group), out_shape=jax.Sh...  136 us
    pallas_call x1, Pallas kernels, kernel_shards(): pl.pallas_call(correlate_kernel, grid=(sub_count * per_dev,), out_shape=j...  15.1 us

profile of v4, /device:TPU:0, one launch (start us, length us, event | category | flops | bytes accessed | tf_op | source)
XLA Modules:
  0.0 152.3 jit_solution(410721083441441071)
XLA Ops:
  0.0 0.0 copy-start
  0.0 0.8 copy-done
  0.8 0.0 copy-start.1
  0.8 0.7 copy-done.1
  1.5 135.7 %spectra.1 = bf16[16,11,128,128]{3,2,1,0:T(8,128)(2,1)S(1)} custom-call(s32[88,256,128]{2,1,0:T(8,128)} %bitcast.7, f32[16,128]{1,0:T(8,128)S(1)} %copy-done.1, f32[128,128]{1,0:T(8,128)S(1)} %copy-done), custom_call_target="tpu_custom_call" | custom-call | tf_op jit(solution)/shard_map/spectra/pallas_call | solution.py:246
  137.3 15.1 %correlate.1 = f32[2,2,4,704,704]{4,3,2,1,0:T(8,128)} custom-call(bf16[8,2,11,8,16,128]{5,4,3,2,1,0:T(8,128)(2,1)S(1)} %bitcast.6), custom_call_target="tpu_custom_call" | custom-call | tf_op jit(solution)/shard_map/correlate/pallas_call | solution.py:271
Async XLA Ops:
  0.0 0.8 copy-start
  0.8 0.7 copy-start.1
